TPU v7x, 512 devices: a whole 4x8x8 slice. The times are simulated.
512 devices in a mesh: gx: 4 (over y_hi), ea: 128 (over y_lo, z, x, core).
Axes of the slice: x: 4, y: 8 (y_hi: 4, y_lo: 2; y = y_hi * 2 + y_lo), z: 8, core: 2. Of those that a mesh axis runs over, the one named last changes fastest.
Arguments:
- ham_diag: float32 [2, 4, 128, 128], P(None, 'gx'), may hold values from -2 to 2, as said below
- ham_coupling: float32 [2, 4, 128, 128], P(None, 'gx'), may hold values from -0.25 to 0.25
- sigma_prev: float32 [2, 4, 128, 128, 128], P(None, 'gx', 'ea'), may hold values from -0.5 to 0.5, as said below
- phonon_form: float32 [128, 128], replicated, may hold values from 0.05 to 0.5
- contact_rate: float32 [2, 128, 128], P(None, 'ea'), may hold values from 0.2 to 2
Outputs:
- sigma_next: float32 [2, 4, 128, 128, 128], P(None, 'gx', 'ea')
Inputs may be any that keep to these rules, and one draw needn't show every extreme that they name: `ham_diag`: each block is Hermitian: real part symmetric, imaginary part antisymmetric. `sigma_prev`: for every block, (S - S^H) / (2 j) is negative definite.
All inputs are finite; a program needn't handle non-finite values.
Results may differ from a plain program's by a relative error of at most 0.0003.
Values sent between devices are 32-bit elements; how exact they have to be, the bound alone decides.
A program may use at most 64 MiB of HBM per device.

v0:
```python
import jax
import jax.numpy as jnp
from jax import lax
from jax.sharding import PartitionSpec as P

BROADENING = 0.05
ENERGY_LOW = -2.0
ENERGY_SPAN = 4.0


def passed_along(block, axis, distance):
    devices = range(lax.axis_size(axis))
    route = [(i - distance, i) for i in devices if i - distance in devices]
    return lax.ppermute(block, axis, route)


def padded(x, sides, width):
    for axis, dim in sides:
        size, length = (lax.axis_size(axis), x.shape[dim])
        up = [(i, (i + 1) % size) for i in range(size - 1)]
        down = [(j, i) for i, j in up]
        last = lax.slice_in_dim(x, length - width, length, axis=dim)
        first = lax.slice_in_dim(x, 0, width, axis=dim)
        before = lax.ppermute(last, axis, up)
        after = lax.ppermute(first, axis, down)
        x = jnp.concatenate([before, x, after], axis=dim)
    return x


def product_real(left, right):
    return jnp.matmul(left, right, precision=lax.Precision.HIGHEST)


def multiply(left, right):
    return (
        product_real(left[0], right[0]) - product_real(left[1], right[1]),
        product_real(left[0], right[1]) + product_real(left[1], right[0]),
    )


def addition(left, right):
    return (left[0] + right[0], left[1] + right[1])


def subtract(left, right):
    return (left[0] - right[0], left[1] - right[1])


def adjoint(pair):
    return (jnp.swapaxes(pair[0], -1, -2), -jnp.swapaxes(pair[1], -1, -2))


def sandwich(left, middle, right):
    return multiply(multiply(left, middle), right)


def pack_pair(pair):
    return jnp.stack([pair[0], pair[1]])


def unpack_pair(stacked):
    return (stacked[0], stacked[1])


def invert(matrix):
    dimension = matrix[0].shape[-1]
    gram_pair = multiply(adjoint(matrix), matrix)
    upper_rows = jnp.concatenate([gram_pair[0], -gram_pair[1]], axis=-1)
    lower_rows = jnp.concatenate([gram_pair[1], gram_pair[0]], axis=-1)
    embedded = jnp.concatenate([upper_rows, lower_rows], axis=-2)
    adjoint_pair = adjoint(matrix)
    right_side = jnp.concatenate([adjoint_pair[0], adjoint_pair[1]], axis=-2)
    factor = jnp.linalg.cholesky(embedded)
    forward_solve = lax.linalg.triangular_solve(factor, right_side, left_side=True, lower=True)
    solution = lax.linalg.triangular_solve(
        factor, forward_solve, left_side=True, lower=True, transpose_a=True
    )
    first_guess = (solution[..., :dimension, :], solution[..., dimension:, :])
    applied = multiply(matrix, first_guess)
    identity = jnp.eye(dimension, dtype=jnp.float32)
    residual = (identity - applied[0], -applied[1])
    return addition(first_guess, multiply(first_guess, residual))


def extend_side(corner, across, pivot_block, transfer, incoming):
    inner_inverse = invert(subtract(pivot_block, incoming))
    return addition(corner, multiply(multiply(across, incoming), multiply(inner_inverse, transfer)))


def per_device(ham_diag, ham_coupling, sigma_prev, phonon_form, contact_rate):
    slices = ham_diag.shape[1]
    energy_count = sigma_prev.shape[2]
    orbitals = ham_diag.shape[-1]
    groups = lax.axis_size("gx")
    position = lax.axis_index("gx")
    energy_total = energy_count * lax.axis_size("ea")
    energy_index = lax.axis_index("ea") * energy_count + jnp.arange(energy_count, dtype=jnp.int32)
    energy = ENERGY_LOW + ENERGY_SPAN * (energy_index.astype(jnp.float32) + 0.5) / energy_total
    identity = jnp.eye(orbitals, dtype=jnp.float32)
    first_flag = (position == 0).astype(jnp.float32)
    last_flag = (position == groups - 1).astype(jnp.float32)
    i = 0
    real_part = energy[:, None, None] * identity - ham_diag[0, i] - sigma_prev[0, i]
    imaginary = BROADENING * identity - ham_diag[1, i] - sigma_prev[1, i]
    imaginary = imaginary + first_flag * contact_rate[0][:, :, None] * identity
    imaginary = imaginary + last_flag * contact_rate[1][:, :, None] * identity
    blocks = [(real_part, imaginary)]
    couplings = [(ham_coupling[0, 0], ham_coupling[1, 0])]
    coupling_out = couplings[slices - 1]
    zeros_block = jnp.zeros((energy_count, orbitals, orbitals), jnp.float32)
    zero_pair = (zeros_block, zeros_block)
    unit_pair = (zeros_block + identity, zeros_block)
    schur_block = blocks[0]
    left_green = [invert(schur_block)]
    corner_last = left_green[slices - 1]
    first_pivot = invert(corner_last)
    toward_last = multiply(first_pivot, corner_last)
    last_to_first = multiply(corner_last, unit_pair)
    reach_left = corner_last
    reach_right = corner_last
    incoming = zero_pair
    outgoing = zero_pair
    for round_index in range(groups - 1):
        outbound = pack_pair(sandwich(adjoint(coupling_out), reach_left, coupling_out))
        incoming = unpack_pair(passed_along(outbound, "gx", 1))
        arrived = unpack_pair(passed_along(pack_pair(reach_right), "gx", -1))
        outgoing = sandwich(coupling_out, arrived, adjoint(coupling_out))
        if round_index < groups - 2:
            reach_left = extend_side(corner_last, last_to_first, first_pivot, toward_last, incoming)
            reach_right = extend_side(corner_last, corner_last, schur_block, unit_pair, outgoing)
    i = 0
    pivot_block = blocks[i]
    pivot_block = subtract(pivot_block, incoming)
    pivot_block = subtract(pivot_block, outgoing)
    green_left = [invert(pivot_block)]
    diagonal = [None] * slices
    diagonal[slices - 1] = green_left[slices - 1]
    whole = jnp.stack([pack_pair(pair) for pair in diagonal], axis=1)
    extended = padded(whole, (("ea", 2),), energy_count)
    return phonon_form * (extended[:, :, :energy_count] + extended[:, :, 2 * energy_count :])


def solution(mesh):
    placed = (
        P(None, "gx", None, None),
        P(None, "gx", None, None),
        P(None, "gx", "ea", None, None),
        P(),
        P(None, "ea", None),
    )
    return jax.shard_map(
        per_device,
        mesh=mesh,
        in_specs=placed,
        out_specs=P(None, "gx", "ea", None, None),
        check_vma=False,
    )
```

profile of v0, /device:TPU:56, one launch (start us, length us, event | category | flops | bytes accessed | tf_op | source)
XLA Modules:
  0.0 532.7 jit_solution(9014562808073716278)
XLA Ops:
  4.1 11.7 %custom-call.46 = f32[1,128,128]{2,1,0:T(8,128)S(1)} custom-call(f32[1,128,128]{2,1,0:T(8,128)S(1)} %cholesky.561), custom_call_target="Cholesky" | custom-call | tf_op jit(solution)/shard_map/jit(cholesky)/cholesky | solution.py:73
  15.9 9.8 %custom-call.47 = f32[1,1,128,128]{2,3,1,0:T(8,128)S(1)} custom-call(f32[1,1,128,128]{3,2,1,0:T(8,128)S(1)} %get-tuple-element.219), custom_call_target="InvertDiagBlocksLowerTriangular" | custom-call | tf_op jit(solution)/shard_map/jit(cholesky)/cholesky | solution.py:73
  26.2 11.7 %custom-call.48 = f32[1,128,128]{2,1,0:T(8,128)S(1)} custom-call(f32[1,128,128]{2,1,0:T(8,128)S(1)} %fusion.49), custom_call_target="Cholesky" | custom-call | tf_op jit(solution)/shard_map/jit(cholesky)/cholesky | solution.py:73
  39.9 4.3 while.28
  44.2 19.7 %custom-call.50 = f32[1,2,128,128]{2,3,1,0:T(8,128)S(1)} custom-call(f32[1,2,128,128]{3,2,1,0:T(8,128)S(1)} %bitcast.1504), custom_call_target="InvertDiagBlocksLowerTriangular" | custom-call | tf_op jit(solution)/shard_map/triangular_solve/custom-call.4 | solution.py:75
  67.6 4.2 collective-permute-start.3
  76.8 11.7 %custom-call.51 = f32[1,128,128]{2,1,0:T(8,128)S(1)} custom-call(f32[1,128,128]{2,1,0:T(8,128)S(1)} %cholesky.564), custom_call_target="Cholesky" | custom-call | tf_op jit(solution)/shard_map/jit(cholesky)/cholesky | solution.py:73
  88.6 9.8 %custom-call.52 = f32[1,1,128,128]{2,3,1,0:T(8,128)S(1)} custom-call(f32[1,1,128,128]{3,2,1,0:T(8,128)S(1)} %get-tuple-element.215), custom_call_target="InvertDiagBlocksLowerTriangular" | custom-call | tf_op jit(solution)/shard_map/jit(cholesky)/cholesky | solution.py:73
  98.9 11.7 %custom-call.53 = f32[1,128,128]{2,1,0:T(8,128)S(1)} custom-call(f32[1,128,128]{2,1,0:T(8,128)S(1)} %fusion.54), custom_call_target="Cholesky" | custom-call | tf_op jit(solution)/shard_map/jit(cholesky)/cholesky | solution.py:73
  113.3 4.0 while.29
  117.3 19.9 %custom-call.55 = f32[1,2,128,128]{2,3,1,0:T(8,128)S(1)} custom-call(f32[1,2,128,128]{3,2,1,0:T(8,128)S(1)} %bitcast.1505), custom_call_target="InvertDiagBlocksLowerTriangular" | custom-call | tf_op jit(solution)/shard_map/triangular_solve/custom-call.4 | solution.py:75
  145.1 11.7 %custom-call.66 = f32[1,128,128]{2,1,0:T(8,128)S(1)} custom-call(f32[1,128,128]{2,1,0:T(8,128)S(1)} %cholesky.573), custom_call_target="Cholesky" | custom-call | tf_op jit(solution)/shard_map/jit(cholesky)/cholesky | solution.py:73
  156.9 9.8 %custom-call.67 = f32[1,1,128,128]{2,3,1,0:T(8,128)S(1)} custom-call(f32[1,1,128,128]{3,2,1,0:T(8,128)S(1)} %get-tuple-element.203), custom_call_target="InvertDiagBlocksLowerTriangular" | custom-call | tf_op jit(solution)/shard_map/jit(cholesky)/cholesky | solution.py:73
  167.2 12.1 %custom-call.68 = f32[1,128,128]{2,1,0:T(8,128)S(1)} custom-call(f32[1,128,128]{2,1,0:T(8,128)S(1)} %fusion.65), custom_call_target="Cholesky" | custom-call | tf_op jit(solution)/shard_map/jit(cholesky)/cholesky | solution.py:73
  181.9 3.9 while.32
  185.8 19.7 %custom-call.70 = f32[1,2,128,128]{2,3,1,0:T(8,128)S(1)} custom-call(f32[1,2,128,128]{3,2,1,0:T(8,128)S(1)} %bitcast.1506), custom_call_target="InvertDiagBlocksLowerTriangular" | custom-call | tf_op jit(solution)/shard_map/triangular_solve/custom-call.4 | solution.py:75
  211.0 11.7 %custom-call.56 = f32[1,128,128]{2,1,0:T(8,128)S(1)} custom-call(f32[1,128,128]{2,1,0:T(8,128)S(1)} %cholesky.567), custom_call_target="Cholesky" | custom-call | tf_op jit(solution)/shard_map/jit(cholesky)/cholesky | solution.py:73
  222.8 9.8 %custom-call.57 = f32[1,1,128,128]{2,3,1,0:T(8,128)S(1)} custom-call(f32[1,1,128,128]{3,2,1,0:T(8,128)S(1)} %get-tuple-element.211), custom_call_target="InvertDiagBlocksLowerTriangular" | custom-call | tf_op jit(solution)/shard_map/jit(cholesky)/cholesky | solution.py:73
  233.1 11.9 %custom-call.58 = f32[1,128,128]{2,1,0:T(8,128)S(1)} custom-call(f32[1,128,128]{2,1,0:T(8,128)S(1)} %fusion.59), custom_call_target="Cholesky" | custom-call | tf_op jit(solution)/shard_map/jit(cholesky)/cholesky | solution.py:73
  247.6 4.0 while.30
  251.6 19.7 %custom-call.60 = f32[1,2,128,128]{2,3,1,0:T(8,128)S(1)} custom-call(f32[1,2,128,128]{3,2,1,0:T(8,128)S(1)} %bitcast.1507), custom_call_target="InvertDiagBlocksLowerTriangular" | custom-call | tf_op jit(solution)/shard_map/triangular_solve/custom-call.4 | solution.py:75
  281.9 5.5 %collective-permute-start.4 = (f32[2,1,128,128]{3,2,1,0:T(8,128)S(1)}, f32[2,1,128,128]{3,2,1,0:T(8,128)S(1)}, u32[]{:S(2)}, u32[]{:S(2)}) collective-permute-start(f32[2,1,128,128]{3,2,1,0:T(8,128)S(1)} %pad_maximum_fusion.4), channel_id=1, source_target_pairs={{128,0},{256,128},{384,256},{129,1},{257,129},{385,257},{130,2},{2... | collective-permute-start | bytes 393224 | tf_op jit(solution)/shard_map/ppermute | solution.py:14
  288.3 1.7 collective-permute-start.1
  293.3 11.7 %custom-call.71 = f32[1,128,128]{2,1,0:T(8,128)S(1)} custom-call(f32[1,128,128]{2,1,0:T(8,128)S(1)} %cholesky.576), custom_call_target="Cholesky" | custom-call | tf_op jit(solution)/shard_map/jit(cholesky)/cholesky | solution.py:73
  305.1 9.8 %custom-call.72 = f32[1,1,128,128]{2,3,1,0:T(8,128)S(1)} custom-call(f32[1,1,128,128]{3,2,1,0:T(8,128)S(1)} %get-tuple-element.199), custom_call_target="InvertDiagBlocksLowerTriangular" | custom-call | tf_op jit(solution)/shard_map/jit(cholesky)/cholesky | solution.py:73
  315.4 11.7 %custom-call.73 = f32[1,128,128]{2,1,0:T(8,128)S(1)} custom-call(f32[1,128,128]{2,1,0:T(8,128)S(1)} %fusion.70), custom_call_target="Cholesky" | custom-call | tf_op jit(solution)/shard_map/jit(cholesky)/cholesky | solution.py:73
  330.0 4.0 while.33
  330.6 1.4 bitcast_dynamic-update-slice_fusion.26
  332.6 1.4 bitcast_dynamic-update-slice_fusion.26
  334.0 19.7 %custom-call.75 = f32[1,2,128,128]{2,3,1,0:T(8,128)S(1)} custom-call(f32[1,2,128,128]{3,2,1,0:T(8,128)S(1)} %bitcast.1508), custom_call_target="InvertDiagBlocksLowerTriangular" | custom-call | tf_op jit(solution)/shard_map/triangular_solve/custom-call.4 | solution.py:75
  358.9 11.7 %custom-call.61 = f32[1,128,128]{2,1,0:T(8,128)S(1)} custom-call(f32[1,128,128]{2,1,0:T(8,128)S(1)} %cholesky.570), custom_call_target="Cholesky" | custom-call | tf_op jit(solution)/shard_map/jit(cholesky)/cholesky | solution.py:73
  370.7 9.8 %custom-call.62 = f32[1,1,128,128]{2,3,1,0:T(8,128)S(1)} custom-call(f32[1,1,128,128]{3,2,1,0:T(8,128)S(1)} %get-tuple-element.207), custom_call_target="InvertDiagBlocksLowerTriangular" | custom-call | tf_op jit(solution)/shard_map/jit(cholesky)/cholesky | solution.py:73
  381.0 11.9 %custom-call.63 = f32[1,128,128]{2,1,0:T(8,128)S(1)} custom-call(f32[1,128,128]{2,1,0:T(8,128)S(1)} %fusion.62), custom_call_target="Cholesky" | custom-call | tf_op jit(solution)/shard_map/jit(cholesky)/cholesky | solution.py:73
  395.7 4.2 while.31
  396.4 1.4 bitcast_dynamic-update-slice_fusion.24
  398.5 1.4 bitcast_dynamic-update-slice_fusion.24
  399.9 19.7 %custom-call.65 = f32[1,2,128,128]{2,3,1,0:T(8,128)S(1)} custom-call(f32[1,2,128,128]{3,2,1,0:T(8,128)S(1)} %bitcast.1509), custom_call_target="InvertDiagBlocksLowerTriangular" | custom-call | tf_op jit(solution)/shard_map/triangular_solve/custom-call.4 | solution.py:75
  429.8 5.5 %collective-permute-start.5 = (f32[2,1,128,128]{3,2,1,0:T(8,128)S(1)}, f32[2,1,128,128]{3,2,1,0:T(8,128)S(1)}, u32[]{:S(2)}, u32[]{:S(2)}) collective-permute-start(f32[2,1,128,128]{3,2,1,0:T(8,128)S(1)} %pad_maximum_fusion.5), channel_id=1, source_target_pairs={{128,0},{256,128},{384,256},{129,1},{257,129},{385,257},{130,2},{2... | collective-permute-start | bytes 393224 | tf_op jit(solution)/shard_map/ppermute | solution.py:14
  436.2 1.7 collective-permute-start.2
  439.5 5.5 %collective-permute-done.2 = f32[2,1,128,128]{2,3,1,0:T(8,128)S(1)} collective-permute-done((f32[2,1,128,128]{2,3,1,0:T(8,128)S(1)}, f32[2,1,128,128]{2,3,1,0:T(8,128)S(1)}, u32[]{:S(2)}, u32[]{:S(2)}) %collective-permute-start.2) | collective-permute-done | bytes 131104 | tf_op jit(solution)/shard_map/ppermute | solution.py:14
  446.7 11.7 %custom-call.76 = f32[1,128,128]{2,1,0:T(8,128)S(1)} custom-call(f32[1,128,128]{2,1,0:T(8,128)S(1)} %cholesky.579), custom_call_target="Cholesky" | custom-call | tf_op jit(solution)/shard_map/jit(cholesky)/cholesky | solution.py:73
  458.5 9.8 %custom-call.77 = f32[1,1,128,128]{2,3,1,0:T(8,128)S(1)} custom-call(f32[1,1,128,128]{3,2,1,0:T(8,128)S(1)} %get-tuple-element.195), custom_call_target="InvertDiagBlocksLowerTriangular" | custom-call | tf_op jit(solution)/shard_map/jit(cholesky)/cholesky | solution.py:73
  468.8 11.7 %custom-call.78 = f32[1,128,128]{2,1,0:T(8,128)S(1)} custom-call(f32[1,128,128]{2,1,0:T(8,128)S(1)} %fusion.75), custom_call_target="Cholesky" | custom-call | tf_op jit(solution)/shard_map/jit(cholesky)/cholesky | solution.py:73
  483.4 4.1 while.34
  487.4 19.7 %custom-call.80 = f32[1,2,128,128]{2,3,1,0:T(8,128)S(1)} custom-call(f32[1,2,128,128]{3,2,1,0:T(8,128)S(1)} %bitcast.1503), custom_call_target="InvertDiagBlocksLowerTriangular" | custom-call | tf_op jit(solution)/shard_map/triangular_solve/custom-call.4 | solution.py:75
  510.8 1.9 collective-permute-start.6
  512.7 16.6 %collective-permute-start.7 = (f32[2,1,1,128,128]{4,3,0,2,1:T(8,128)S(1)}, f32[2,1,1,128,128]{4,3,0,2,1:T(8,128)S(1)}, u32[]{:S(2)}, u32[]{:S(2)}) collective-permute-start(f32[2,1,1,128,128]{4,3,0,2,1:T(8,128)S(1)} %maximum_bitcast_fusion), channel_id=1, source_target_pairs={{1,0},{2,1},{3,2},{4,3},{5,4},{6,5},{7,6},{8,7},{9,8},{10,9},{11,1... | collective-permute-start | bytes 393224 | tf_op jit(solution)/shard_map/ppermute | solution.py:25
  530.0 1.8 collective-permute-done.7
  (402 shorter events, 99.4 us)
Async XLA Ops:
  0.9 0.9 copy-start.1
  1.8 0.7 copy-start.3
  67.5 4.2 copy-start
  67.6 74.2 %collective-permute-start.3 = (f32[2,1,128,128]{3,2,1,0:T(8,128)S(1)}, f32[2,1,128,128]{3,2,1,0:T(8,128)S(1)}, u32[]{:S(2)}, u32[]{:S(2)}) collective-permute-start(f32[2,1,128,128]{3,2,1,0:T(8,128)S(1)} %pad_maximum_fusion.3), channel_id=1, source_target_pairs={{128,0},{256,128},{384,256},{129,1},{257,129},{385,257},{130,2},{2... | collective-permute-start | bytes 393224 | tf_op jit(solution)/shard_map/ppermute | solution.py:14
  74.1 135.2 %collective-permute-start = (f32[2,1,128,128]{3,2,1,0:T(8,128)S(1)}, f32[2,1,128,128]{3,2,1,0:T(8,128)S(1)}, u32[]{:S(2)}, u32[]{:S(2)}) collective-permute-start(f32[2,1,128,128]{3,2,1,0:T(8,128)S(1)} %pad_maximum_fusion), channel_id=1, source_target_pairs={{0,128},{128,256},{256,384},{1,129},{129,257},{257,385},{2,130},{1... | collective-permute-start | bytes 393224 | tf_op jit(solution)/shard_map/ppermute | solution.py:14
  281.9 8.1 %collective-permute-start.4 = (f32[2,1,128,128]{3,2,1,0:T(8,128)S(1)}, f32[2,1,128,128]{3,2,1,0:T(8,128)S(1)}, u32[]{:S(2)}, u32[]{:S(2)}) collective-permute-start(f32[2,1,128,128]{3,2,1,0:T(8,128)S(1)} %pad_maximum_fusion.4), channel_id=1, source_target_pairs={{128,0},{256,128},{384,256},{129,1},{257,129},{385,257},{130,2},{2... | collective-permute-start | bytes 393224 | tf_op jit(solution)/shard_map/ppermute | solution.py:14
  288.3 69.2 %collective-permute-start.1 = (f32[2,1,128,128]{3,2,1,0:T(8,128)S(1)}, f32[2,1,128,128]{3,2,1,0:T(8,128)S(1)}, u32[]{:S(2)}, u32[]{:S(2)}) collective-permute-start(f32[2,1,128,128]{3,2,1,0:T(8,128)S(1)} %pad_maximum_fusion.1), channel_id=1, source_target_pairs={{0,128},{128,256},{256,384},{1,129},{129,257},{257,385},{2,130},{1... | collective-permute-start | bytes 393224 | tf_op jit(solution)/shard_map/ppermute | solution.py:14
  429.8 8.1 %collective-permute-start.5 = (f32[2,1,128,128]{3,2,1,0:T(8,128)S(1)}, f32[2,1,128,128]{3,2,1,0:T(8,128)S(1)}, u32[]{:S(2)}, u32[]{:S(2)}) collective-permute-start(f32[2,1,128,128]{3,2,1,0:T(8,128)S(1)} %pad_maximum_fusion.5), channel_id=1, source_target_pairs={{128,0},{256,128},{384,256},{129,1},{257,129},{385,257},{130,2},{2... | collective-permute-start | bytes 393224 | tf_op jit(solution)/shard_map/ppermute | solution.py:14
  436.2 8.8 %collective-permute-start.2 = (f32[2,1,128,128]{2,3,1,0:T(8,128)S(1)}, f32[2,1,128,128]{2,3,1,0:T(8,128)S(1)}, u32[]{:S(2)}, u32[]{:S(2)}) collective-permute-start(f32[2,1,128,128]{2,3,1,0:T(8,128)S(1)} %pad_maximum_fusion.2), channel_id=1, source_target_pairs={{0,128},{128,256},{256,384},{1,129},{129,257},{257,385},{2,130},{1... | collective-permute-start | bytes 393224 | tf_op jit(solution)/shard_map/ppermute | solution.py:14
  510.8 21.0 %copy-start.2 = (f32[128,128]{1,0:T(8,128)S(1)}, f32[128,128]{1,0:T(8,128)}, u32[]{:S(2)}) copy-start(f32[128,128]{1,0:T(8,128)} %param.13) | copy-start | bytes 196612
  510.8 19.2 %collective-permute-start.6 = (f32[2,1,1,128,128]{4,3,0,2,1:T(8,128)S(1)}, f32[2,1,1,128,128]{4,3,0,2,1:T(8,128)S(1)}, u32[]{:S(2)}, u32[]{:S(2)}) collective-permute-start(f32[2,1,1,128,128]{4,3,0,2,1:T(8,128)S(1)} %maximum_bitcast_fusion), channel_id=1, source_target_pairs={{0,1},{1,2},{2,3},{3,4},{4,5},{5,6},{6,7},{7,8},{8,9},{9,10},{10,1... | collective-permute-start | bytes 393224 | tf_op jit(solution)/shard_map/ppermute | solution.py:24
  512.7 19.1 %collective-permute-start.7 = (f32[2,1,1,128,128]{4,3,0,2,1:T(8,128)S(1)}, f32[2,1,1,128,128]{4,3,0,2,1:T(8,128)S(1)}, u32[]{:S(2)}, u32[]{:S(2)}) collective-permute-start(f32[2,1,1,128,128]{4,3,0,2,1:T(8,128)S(1)} %maximum_bitcast_fusion), channel_id=1, source_target_pairs={{1,0},{2,1},{3,2},{4,3},{5,4},{6,5},{7,6},{8,7},{9,8},{10,9},{11,1... | collective-permute-start | bytes 393224 | tf_op jit(solution)/shard_map/ppermute | solution.py:25
where the time goes:
time: 541 us; the launch traced here: 533 us
  other arithmetic  382 us (71%)
  matrix products  60.3 us (11%)
  starting transfers between devices  38.3 us (7%)
  local copies, waits for them, and re-layouts  31.5 us (6%)
  between operations  11.5 us (2%)
  waiting for transfers between devices  7.98 us (1%)
    another operation x48, other arithmetic, invert(): factor = jnp.linalg.cholesky(embedded)  243 us
    another operation x15, other arithmetic, invert(): lax.linalg.triangular_solve(factor, forward_solve, left_side=True, lower=...  138 us
    dot_general x188, matrix products, product_real(): return jnp.matmul(left, right, precision=lax.Precision.HIGHEST)  46.5 us
    another operation x50, local copies, waits for them, and re-layouts, invert(): lax.linalg.triangular_solve(factor, forward_solve, left_side=True, lower=...  27.8 us
    ppermute x6, starting transfers between devices, passed_along(): return lax.ppermute(block, axis, route)  19.8 us
    ppermute x1, starting transfers between devices, padded(): after = lax.ppermute(first, axis, down)  16.6 us
  transfers between devices with their start and end apart: 8, of which 3 were waited for; matrix products, arithmetic and copies ran while one was open for 38% of the time, Pallas kernels for 0%

commit v1 on v0

v1 whole, which is shorter than its diff:
```python
import jax
import jax.numpy as jnp
from jax import lax
from jax.experimental import pallas as pl
from jax.experimental.pallas import tpu as pltpu
from jax.sharding import PartitionSpec as P

BROADENING = 0.05
ENERGY_LOW = -2.0
ENERGY_SPAN = 4.0
N = 128
TILE = (8, 128)
MESH = pl.DeviceIdType.MESH


def spread(x):
    return jnp.broadcast_to(x, TILE)


def split3(x):
    high = x.astype(jnp.bfloat16)
    rest = x - high.astype(jnp.float32)
    middle = rest.astype(jnp.bfloat16)
    low = (rest - middle.astype(jnp.float32)).astype(jnp.bfloat16)
    return high, middle, low


def dot16(a, b):
    return jnp.dot(a, b, preferred_element_type=jnp.float32)


def product6(left, right):
    lh, lm, ll = left
    rh, rm, rl = right
    small = (dot16(lm, rm) + dot16(lh, rl)) + dot16(ll, rh)
    return dot16(lh, rh) + ((dot16(lh, rm) + dot16(lm, rh)) + small)


def multiply(left, right):
    x = jnp.concatenate(left, axis=1)
    top = jnp.concatenate(right, axis=1)
    bottom = jnp.concatenate([-right[1], right[0]], axis=1)
    y = product6(split3(x), split3(jnp.concatenate([top, bottom], axis=0)))
    return y[:, :N], y[:, N:]


def adjoint(pair):
    return pair[0].T, -pair[1].T


def addition(left, right):
    return left[0] + right[0], left[1] + right[1]


def subtract(left, right):
    return left[0] - right[0], left[1] - right[1]


def pair_of(ref):
    return ref[0], ref[1]


def store(ref, pair):
    ref[0] = pair[0]
    ref[1] = pair[1]


def pivot_rows(t, rows):
    sub = lax.broadcasted_iota(jnp.int32, TILE, 0)
    lane = lax.broadcasted_iota(jnp.int32, TILE, 1)
    o = 8 * t
    cols = [(spread(rows[0][:, o + m : o + m + 1]), spread(rows[1][:, o + m : o + m + 1])) for m in range(8)]
    inside = (lane >= o) & (lane < o + 8)
    x = (
        jnp.where(inside, jnp.where(lane - o == sub, 1.0, 0.0), rows[0]),
        jnp.where(inside, 0.0, rows[1]),
    )
    for k in range(8):
        at = sub == k
        mr, mi = cols[k]
        pr, pi = spread(mr[k : k + 1]), spread(mi[k : k + 1])
        recip = 1.0 / (pr * pr + pi * pi)
        mr, mi = jnp.where(at, -1.0, mr), jnp.where(at, 0.0, mi)
        ur, ui = mr * pr + mi * pi, mi * pr - mr * pi
        wr, wi = ur * recip, ui * recip

        def step(v, next_pivot):
            rr, ri = spread(v[0][k : k + 1]), spread(v[1][k : k + 1])
            vr, vi = jnp.where(at, 0.0, v[0]), jnp.where(at, 0.0, v[1])
            if next_pivot:
                return vr - (ur * rr - ui * ri) * recip, vi - (ur * ri + ui * rr) * recip
            return vr - (wr * rr - wi * ri), vi - (wr * ri + wi * rr)

        for m in range(k + 1, 8):
            cols[m] = step(cols[m], m == k + 1)
        x = step(x, False)
    return x


def eliminate(rows, t, x):
    lane = lax.broadcasted_iota(jnp.int32, TILE, 1)
    o = 8 * t
    inside = (lane >= o) & (lane < o + 8)
    real, imag = [], []
    for k in range(8):
        cr, ci = spread(rows[0][:, o + k : o + k + 1]), spread(rows[1][:, o + k : o + k + 1])
        rr, ri = spread(x[0][k : k + 1]), spread(x[1][k : k + 1])
        real.append(cr * rr - ci * ri)
        imag.append(cr * ri + ci * rr)
    while len(real) > 1:
        real = [a + b for a, b in zip(real[::2], real[1::2])]
        imag = [a + b for a, b in zip(imag[::2], imag[1::2])]
    return jnp.where(inside, 0.0, rows[0]) - real[0], jnp.where(inside, 0.0, rows[1]) - imag[0]


def invert(ref):
    groups = N // 8
    a = [(ref[0, 8 * g : 8 * g + 8, :], ref[1, 8 * g : 8 * g + 8, :]) for g in range(groups)]
    lane = lax.broadcasted_iota(jnp.int32, TILE, 1)
    for s in range(groups // 2):
        g0, g1 = 2 * s, 2 * s + 1
        ahead = [] if s == groups // 2 - 1 else [g1 + 1, g1 + 2]
        old = list(a)
        x0 = pivot_rows(g0, a[g0])
        second = eliminate(a[g1], g0, x0)
        early = [eliminate(a[h], g0, x0) for h in ahead]
        x1 = pivot_rows(g1, second)
        early = [eliminate(h, g1, x1) for h in early]
        x0 = eliminate(x0, g1, x1)
        a[g0], a[g1] = x0, x1
        for h, v in zip(ahead, early):
            a[h] = v
        done = [g0, g1] + ahead
        real = jnp.concatenate([x0[0], x1[0]], axis=0)
        imag = jnp.concatenate([x0[1], x1[1]], axis=0)
        top = split3(jnp.concatenate([real, imag], axis=1))
        bottom = split3(jnp.concatenate([-imag, real], axis=1))

        def placed(x):
            above = [jnp.zeros((16 * s, 2 * N), jnp.bfloat16)] if s else []
            below = [jnp.zeros((N - 16 * s - 16, 2 * N), jnp.bfloat16)] if ahead else []
            return above + [x] + below

        right = [jnp.concatenate(placed(u) + placed(v), axis=0) for u, v in zip(top, bottom)]
        left = jnp.concatenate(
            [jnp.concatenate([v[0] for v in old], axis=0), jnp.concatenate([v[1] for v in old], axis=0)], axis=1
        )
        change = product6(split3(left), right)
        inside = (lane >= 16 * s) & (lane < 16 * s + 16)
        for g in range(groups):
            if g not in done:
                rows = slice(8 * g, 8 * g + 8)
                a[g] = (
                    jnp.where(inside, 0.0, old[g][0]) - change[rows, :N],
                    jnp.where(inside, 0.0, old[g][1]) - change[rows, N:],
                )
    for g in range(groups):
        ref[0, 8 * g : 8 * g + 8, :] = a[g][0]
        ref[1, 8 * g : 8 * g + 8, :] = a[g][1]


def kernel(
    diag_ref, coupling_ref, sigma_ref, form_ref, rate_ref, out_ref,
    own, work, near, link, mid, link_h, one, gv, vg, sent, far, last, before, after,
    send_sem, recv_sem,
):
    gx = lax.axis_index("gx")
    ea = lax.axis_index("ea")
    count = lax.axis_size("ea")
    left = gx < 2
    outer = (gx == 0) | (gx == 3)
    inner = jnp.logical_not(outer)
    partner = gx + 1 - 2 * lax.rem(gx, 2)
    across = 3 - gx
    beyond = lax.rem(gx + 2, 4)

    def copy(src, dst, at, to_gx, to_ea, landed=None):
        return pltpu.make_async_remote_copy(
            src_ref=src,
            dst_ref=dst,
            send_sem=send_sem.at[at],
            recv_sem=recv_sem.at[at if landed is None else landed],
            device_id=(to_gx, to_ea),
            device_id_type=MESH,
        )

    send_near = copy(own, near, 0, partner, ea)
    send_link = copy(coupling_ref.at[:, 0], link, 1, partner, ea)
    send_mid = copy(sent, mid, 2, partner, ea)
    send_across = copy(sent, far, 3, across, ea)
    send_beyond = copy(sent, far, 4, beyond, ea, 3)
    send_up = copy(last, before, 5, gx, lax.rem(ea + 1, count))
    send_down = copy(last, after, 6, gx, lax.rem(ea + count - 1, count))

    barrier = pltpu.get_barrier_semaphore()

    def greet(to_gx, to_ea):
        pl.semaphore_signal(barrier, inc=1, device_id=(to_gx, to_ea), device_id_type=MESH)

    greet(partner, ea)
    greet(beyond, ea)

    @pl.when(outer)
    def _():
        greet(across, ea)

    @pl.when(ea > 0)
    def _():
        greet(gx, ea - 1)

    @pl.when(ea < count - 1)
    def _():
        greet(gx, ea + 1)

    row = lax.broadcasted_iota(jnp.int32, (N, N), 0)
    column = lax.broadcasted_iota(jnp.int32, (N, N), 1)
    energy = ENERGY_LOW + ENERGY_SPAN * (ea.astype(jnp.float32) + 0.5) / count
    first = jnp.where(gx == 0, 1.0, 0.0)
    final = jnp.where(gx == 3, 1.0, 0.0)
    rate = BROADENING + (first * rate_ref[0] + final * rate_ref[1])
    on_diagonal = row == column
    own[0] = jnp.where(on_diagonal, energy, 0.0) - diag_ref[0, 0] - sigma_ref[0, 0, 0]
    own[1] = jnp.where(on_diagonal, rate, 0.0) - diag_ref[1, 0] - sigma_ref[1, 0, 0]

    waits = jnp.where(outer, 3, 2) + jnp.where(ea > 0, 1, 0) + jnp.where(ea < count - 1, 1, 0)

    @pl.when(inner)
    def _():
        pl.semaphore_wait(barrier, waits)
        send_near.start()
        send_link.start()

    @pl.when(outer)
    def _():
        work[...] = own[...]

    def level(number, carry):
        @pl.when(outer | (number == 2))
        def _():
            invert(work)

        @pl.when(outer & (number == 0))
        def _():
            pl.semaphore_wait(barrier, waits)
            send_near.wait_recv()
            send_link.wait_recv()

            @pl.when(left)
            def _():
                store(link_h, (coupling_ref[0, 0], coupling_ref[1, 0]))
                store(one, adjoint(pair_of(link_h)))

            @pl.when(jnp.logical_not(left))
            def _():
                store(one, pair_of(link))
                store(link_h, adjoint(pair_of(link)))

            g = pair_of(work)
            store(own, g)
            reached = multiply(pair_of(one), g)
            store(vg, reached)
            pivot = subtract(pair_of(near), multiply(reached, pair_of(link_h)))
            store(work, pivot)
            store(sent, pivot)
            send_mid.start()
            store(mid, pivot)
            store(gv, multiply(g, pair_of(link_h)))

        @pl.when(outer & (number == 1))
        def _():
            send_mid.wait_send()

            @pl.when(left)
            def _():
                u = pair_of(link)
                store(sent, multiply(adjoint(u), multiply(pair_of(work), u)))

            @pl.when(jnp.logical_not(left))
            def _():
                store(sent, pair_of(work))

            send_across.start()
            send_beyond.start()
            send_across.wait_recv()

        @pl.when(inner & (number == 1))
        def _():
            send_mid.wait_recv()
            send_beyond.wait_recv()
            store(link, (coupling_ref[0, 0], coupling_ref[1, 0]))

        @pl.when(number == 1)
        def _():
            @pl.when(left)
            def _():
                u = pair_of(link)
                store(far, multiply(multiply(u, pair_of(far)), adjoint(u)))

            store(work, subtract(pair_of(mid), pair_of(far)))

        return carry

    lax.fori_loop(0, 3, level, 0)

    @pl.when(outer)
    def _():
        store(last, addition(pair_of(own), multiply(multiply(pair_of(gv), pair_of(work)), pair_of(vg))))

    @pl.when(inner)
    def _():
        store(last, pair_of(work))

    @pl.when(ea < count - 1)
    def _():
        send_up.start()

    @pl.when(ea > 0)
    def _():
        send_down.start()

    @pl.when(ea == 0)
    def _():
        before[...] = jnp.zeros_like(before)

    @pl.when(ea == count - 1)
    def _():
        after[...] = jnp.zeros_like(after)

    @pl.when(inner)
    def _():
        send_near.wait_send()
        send_link.wait_send()

    @pl.when(outer)
    def _():
        send_across.wait_send()
        send_beyond.wait_send()

    @pl.when(ea > 0)
    def _():
        send_up.wait_recv()

    @pl.when(ea < count - 1)
    def _():
        send_down.wait_recv()

    for c in range(2):
        out_ref[c, 0, 0] = form_ref[...] * (before[c] + after[c])

    @pl.when(ea < count - 1)
    def _():
        send_up.wait_send()

    @pl.when(ea > 0)
    def _():
        send_down.wait_send()


def per_device(ham_diag, ham_coupling, sigma_prev, phonon_form, contact_rate):
    block = pltpu.VMEM((2, N, N), jnp.float32)
    return pl.pallas_call(
        kernel,
        out_shape=jax.ShapeDtypeStruct(sigma_prev.shape, jnp.float32),
        in_specs=[pl.BlockSpec(memory_space=pltpu.VMEM)] * 5,
        out_specs=pl.BlockSpec(memory_space=pltpu.VMEM),
        scratch_shapes=[block] * 14
        + [pltpu.SemaphoreType.DMA((7,)), pltpu.SemaphoreType.DMA((7,))],
        compiler_params=pltpu.CompilerParams(
            collective_id=0, has_side_effects=True, vmem_limit_bytes=48 << 20
        ),
        name="born_update",
    )(ham_diag, ham_coupling, sigma_prev, phonon_form, contact_rate)


def solution(mesh):
    placed = (
        P(None, "gx", None, None),
        P(None, "gx", None, None),
        P(None, "gx", "ea", None, None),
        P(),
        P(None, "ea", None),
    )
    return jax.shard_map(
        per_device,
        mesh=mesh,
        in_specs=placed,
        out_specs=P(None, "gx", "ea", None, None),
        check_vma=False,
    )
```

time: 541 us -> 55 us (0.10)
  the two profiles are of different devices: /device:TPU:56 before, /device:TPU:40 now
where the time goes in v1:
time: 55 us; the launch traced here: 54.8 us
  Pallas kernels  49.9 us (91%)
  local copies, waits for them, and re-layouts  4.89 us (9%)
    pallas_call x1, Pallas kernels, per_device(): pl.pallas_call(kernel, out_shape=jax.ShapeDtypeStruct(sigma_prev.shape, j...  49.9 us
    unnamed x11, local copies, waits for them, and re-layouts  4.89 us

profile of v1, /device:TPU:40, one launch (start us, length us, event | category | flops | bytes accessed | tf_op | source)
XLA Modules:
  0.0 54.8 jit_solution(12484910121074124509)
XLA Ops:
  0.0 0.0 copy-start
  0.0 0.9 %copy-done = f32[2,1,128,128]{3,2,1,0:T(8,128)S(1)} copy-done((f32[2,1,128,128]{3,2,1,0:T(8,128)S(1)}, f32[2,1,128,128]{3,2,1,0:T(8,128)}, u32[]{:S(2)}) %copy-start) | copy-done | bytes 131096
  0.9 0.0 copy-start.1
  0.9 0.9 %copy-done.1 = f32[2,1,128,128]{3,2,1,0:T(8,128)S(1)} copy-done((f32[2,1,128,128]{3,2,1,0:T(8,128)S(1)}, f32[2,1,128,128]{3,2,1,0:T(8,128)}, u32[]{:S(2)}) %copy-start.1) | copy-done | bytes 131096
  1.8 0.0 copy-start.2
  1.8 0.9 %copy-done.2 = f32[2,1,1,128,128]{4,3,2,1,0:T(8,128)S(1)} copy-done((f32[2,1,1,128,128]{4,3,2,1,0:T(8,128)S(1)}, f32[2,1,1,128,128]{4,3,2,1,0:T(8,128)}, u32[]{:S(2)}) %copy-start.2) | copy-done | bytes 131096
  2.7 0.0 copy-start.3
  2.7 0.8 %copy-done.3 = f32[128,128]{1,0:T(8,128)S(1)} copy-done((f32[128,128]{1,0:T(8,128)S(1)}, f32[128,128]{1,0:T(8,128)}, u32[]{:S(2)}) %copy-start.3) | copy-done | bytes 65560
  3.6 0.0 copy-start.4
  3.6 0.7 %copy-done.4 = f32[2,1,128]{2,1,0:T(1,128)S(1)} copy-done((f32[2,1,128]{2,1,0:T(1,128)S(1)}, f32[2,1,128]{2,1,0:T(1,128)}, u32[]{:S(2)}) %copy-start.4) | copy-done | bytes 1048
  4.2 49.9 %born_update.1 = f32[2,1,1,128,128]{4,3,2,1,0:T(8,128)S(1)} custom-call(f32[2,1,128,128]{3,2,1,0:T(8,128)S(1)} %copy-done, f32[2,1,128,128]{3,2,1,0:T(8,128)S(1)} %copy-done.1, f32[2,1,1,128,128]{4,3,2,1,0:T(8,128)S(1)} %copy-done.2, f32[128,128]{1,0:T(8,128)S(1)} %copy-done.3, f32[2,1,128]{2,1,0:T(1,128)S(1)} %copy-done.4), custom_call_target="tpu_custom_call" | custom-call | tf_op jit(solution)/shard_map/born_update/pallas_call | solution.py:361
  54.2 0.7 %copy.7 = f32[2,1,1,128,128]{4,3,2,1,0:T(8,128)} copy(f32[2,1,1,128,128]{4,3,2,1,0:T(8,128)S(1)} %born_update.1) | data formatting | bytes 262144
Async XLA Ops:
  0.0 0.9 %copy-start = (f32[2,1,128,128]{3,2,1,0:T(8,128)S(1)}, f32[2,1,128,128]{3,2,1,0:T(8,128)}, u32[]{:S(2)}) copy-start(f32[2,1,128,128]{3,2,1,0:T(8,128)} %diag_ref.1) | copy-start | bytes 393220
  0.9 0.9 %copy-start.1 = (f32[2,1,128,128]{3,2,1,0:T(8,128)S(1)}, f32[2,1,128,128]{3,2,1,0:T(8,128)}, u32[]{:S(2)}) copy-start(f32[2,1,128,128]{3,2,1,0:T(8,128)} %coupling_ref.1) | copy-start | bytes 393220
  1.8 0.9 %copy-start.2 = (f32[2,1,1,128,128]{4,3,2,1,0:T(8,128)S(1)}, f32[2,1,1,128,128]{4,3,2,1,0:T(8,128)}, u32[]{:S(2)}) copy-start(f32[2,1,1,128,128]{4,3,2,1,0:T(8,128)} %sigma_ref.1) | copy-start | bytes 393220
  2.7 0.8 %copy-start.3 = (f32[128,128]{1,0:T(8,128)S(1)}, f32[128,128]{1,0:T(8,128)}, u32[]{:S(2)}) copy-start(f32[128,128]{1,0:T(8,128)} %form_ref.1) | copy-start | bytes 196612
  3.6 0.7 %copy-start.4 = (f32[2,1,128]{2,1,0:T(1,128)S(1)}, f32[2,1,128]{2,1,0:T(1,128)}, u32[]{:S(2)}) copy-start(f32[2,1,128]{2,1,0:T(1,128)} %rate_ref.1) | copy-start | bytes 3076

commit v2 on v1

v2 whole, which is shorter than its diff:
```python
import jax
import jax.numpy as jnp
from jax import lax
from jax.experimental import pallas as pl
from jax.experimental.pallas import tpu as pltpu
from jax.sharding import PartitionSpec as P

BROADENING = 0.05
ENERGY_LOW = -2.0
ENERGY_SPAN = 4.0
N = 128
TILE = (8, 128)
SHARE = 8
ROWS = N // SHARE
MESH = pl.DeviceIdType.MESH


def spread(x):
    return jnp.broadcast_to(x, TILE)


def split3(x):
    high = x.astype(jnp.bfloat16)
    rest = x - high.astype(jnp.float32)
    middle = rest.astype(jnp.bfloat16)
    low = (rest - middle.astype(jnp.float32)).astype(jnp.bfloat16)
    return high, middle, low


def dot16(a, b):
    return jnp.dot(a, b, preferred_element_type=jnp.float32)


def product6(left, right):
    lh, lm, ll = left
    rh, rm, rl = right
    small = (dot16(lm, rm) + dot16(lh, rl)) + dot16(ll, rh)
    return dot16(lh, rh) + ((dot16(lh, rm) + dot16(lm, rh)) + small)


def multiply(left, right):
    x = jnp.concatenate(left, axis=1)
    top = jnp.concatenate(right, axis=1)
    bottom = jnp.concatenate([-right[1], right[0]], axis=1)
    y = product6(split3(x), split3(jnp.concatenate([top, bottom], axis=0)))
    return y[:, :N], y[:, N:]


def adjoint(pair):
    return pair[0].T, -pair[1].T


def addition(left, right):
    return left[0] + right[0], left[1] + right[1]


def subtract(left, right):
    return left[0] - right[0], left[1] - right[1]


def pair_of(ref):
    return ref[0], ref[1]


def store(ref, pair):
    ref[0] = pair[0]
    ref[1] = pair[1]


def pivot_rows(t, rows):
    sub = lax.broadcasted_iota(jnp.int32, TILE, 0)
    lane = lax.broadcasted_iota(jnp.int32, TILE, 1)
    o = 8 * t
    cols = [(spread(rows[0][:, o + m : o + m + 1]), spread(rows[1][:, o + m : o + m + 1])) for m in range(8)]
    inside = (lane >= o) & (lane < o + 8)
    x = (
        jnp.where(inside, jnp.where(lane - o == sub, 1.0, 0.0), rows[0]),
        jnp.where(inside, 0.0, rows[1]),
    )
    for k in range(8):
        at = sub == k
        mr, mi = cols[k]
        pr, pi = spread(mr[k : k + 1]), spread(mi[k : k + 1])
        recip = 1.0 / (pr * pr + pi * pi)
        mr, mi = jnp.where(at, -1.0, mr), jnp.where(at, 0.0, mi)
        ur, ui = mr * pr + mi * pi, mi * pr - mr * pi
        wr, wi = ur * recip, ui * recip

        def step(v, next_pivot):
            rr, ri = spread(v[0][k : k + 1]), spread(v[1][k : k + 1])
            vr, vi = jnp.where(at, 0.0, v[0]), jnp.where(at, 0.0, v[1])
            if next_pivot:
                return vr - (ur * rr - ui * ri) * recip, vi - (ur * ri + ui * rr) * recip
            return vr - (wr * rr - wi * ri), vi - (wr * ri + wi * rr)

        for m in range(k + 1, 8):
            cols[m] = step(cols[m], m == k + 1)
        x = step(x, False)
    return x


def factors(rows, t):
    o = 8 * t
    return [(spread(rows[0][:, o + k : o + k + 1]), spread(rows[1][:, o + k : o + k + 1])) for k in range(8)]


def combine(columns, x):
    real, imag = [], []
    for k, (cr, ci) in enumerate(columns):
        rr, ri = spread(x[0][k : k + 1]), spread(x[1][k : k + 1])
        real.append(cr * rr - ci * ri)
        imag.append(cr * ri + ci * rr)
    while len(real) > 1:
        real = [a + b for a, b in zip(real[::2], real[1::2])]
        imag = [a + b for a, b in zip(imag[::2], imag[1::2])]
    return real[0], imag[0]


def cleared(rows, first, width):
    lane = lax.broadcasted_iota(jnp.int32, TILE, 1)
    inside = (lane >= first) & (lane < first + width)
    return jnp.where(inside, 0.0, rows[0]), jnp.where(inside, 0.0, rows[1])


def invert(ref, halfway):
    groups = N // 8
    a = [(ref[0, 8 * g : 8 * g + 8, :], ref[1, 8 * g : 8 * g + 8, :]) for g in range(groups)]
    for s in range(groups // 2):
        if s == 4:
            halfway()
        g0, g1 = 2 * s, 2 * s + 1
        ahead = [] if s == groups // 2 - 1 else [g1 + 1, g1 + 2]
        old = list(a)
        x0 = pivot_rows(g0, a[g0])
        x1 = pivot_rows(g1, subtract(cleared(a[g1], 8 * g0, 8), combine(factors(a[g1], g0), x0)))
        x0 = subtract(cleared(x0, 8 * g1, 8), combine(factors(x0, g1), x1))
        for h in ahead:
            part = subtract(cleared(old[h], 16 * s, 16), combine(factors(old[h], g1), x1))
            a[h] = subtract(part, combine(factors(old[h], g0), x0))
        a[g0], a[g1] = x0, x1
        done = [g0, g1] + ahead
        real = jnp.concatenate([x0[0], x1[0]], axis=0)
        imag = jnp.concatenate([x0[1], x1[1]], axis=0)
        top = split3(jnp.concatenate([real, imag], axis=1))
        bottom = split3(jnp.concatenate([-imag, real], axis=1))

        def placed(x):
            above = [jnp.zeros((16 * s, 2 * N), jnp.bfloat16)] if s else []
            below = [jnp.zeros((N - 16 * s - 16, 2 * N), jnp.bfloat16)] if ahead else []
            return above + [x] + below

        right = [jnp.concatenate(placed(u) + placed(v), axis=0) for u, v in zip(top, bottom)]
        left = jnp.concatenate(
            [jnp.concatenate([v[0] for v in old], axis=0), jnp.concatenate([v[1] for v in old], axis=0)], axis=1
        )
        change = product6(split3(left), right)
        for g in range(groups):
            if g not in done:
                rows = slice(8 * g, 8 * g + 8)
                a[g] = subtract(cleared(old[g], 16 * s, 16), (change[rows, :N], change[rows, N:]))
    for g in range(groups):
        ref[0, 8 * g : 8 * g + 8, :] = a[g][0]
        ref[1, 8 * g : 8 * g + 8, :] = a[g][1]


def kernel(
    diag_hbm, coupling_hbm, sigma_hbm, form_hbm, rate_hbm, out_ref,
    diag, coupling, sigma, form, rates,
    own, work, near, link, mid, bridge, bridge_h, step_in, step_out, reached, sent, far, last, before, after,
    load_sem, send_sem, recv_sem, pass_sem, piece_sem,
):
    gx = lax.axis_index("gx")
    ea = lax.axis_index("ea")
    count = lax.axis_size("ea")
    left = gx < 2
    right = jnp.logical_not(left)
    outer = (gx == 0) | (gx == 3)
    inner = jnp.logical_not(outer)
    even = lax.rem(gx, 2) == 0
    odd = jnp.logical_not(even)
    partner = gx + 1 - 2 * lax.rem(gx, 2)
    across = 3 - gx
    place = lax.rem(ea, SHARE)
    base = ea - place

    def load(at, src, dst):
        return pltpu.make_async_copy(src, dst, load_sem.at[at])

    load_diag = load(0, diag_hbm, diag)
    load_sigma = load(1, sigma_hbm, sigma)
    load_rates = load(2, rate_hbm, rates)
    load_coupling = load(3, coupling_hbm, coupling)
    load_form = load(4, form_hbm, form)
    for one_load in (load_diag, load_sigma, load_rates, load_coupling, load_form):
        one_load.start()

    def copy(src, dst, at, to_gx, to_ea):
        return pltpu.make_async_remote_copy(
            src_ref=src,
            dst_ref=dst,
            send_sem=send_sem.at[at],
            recv_sem=recv_sem.at[at],
            device_id=(to_gx, to_ea),
            device_id_type=MESH,
        )

    def piece(ref, index):
        return ref.at[:, pl.ds(pl.multiple_of(index * ROWS, ROWS), ROWS), :]

    send_near = copy(own, near, 0, partner, ea)
    send_piece = copy(piece(coupling.at[:, 0], place), piece(link, place), 1, partner, ea)
    send_mid = copy(sent, mid, 2, partner, ea)
    send_across = copy(sent, far, 3, across, ea)
    send_up = copy(last, before, 4, gx, lax.rem(ea + 1, count))
    send_down = copy(last, after, 5, gx, lax.rem(ea + count - 1, count))

    def hand_on(step, owner):
        return pltpu.make_async_remote_copy(
            src_ref=piece(link, owner),
            dst_ref=piece(link, owner),
            send_sem=pass_sem.at[step],
            recv_sem=piece_sem.at[step],
            device_id=(gx, base + lax.rem(place + step, SHARE)),
            device_id_type=MESH,
        )

    barrier = pltpu.get_barrier_semaphore()

    def greet(to_gx, to_ea):
        pl.semaphore_signal(barrier, inc=1, device_id=(to_gx, to_ea), device_id_type=MESH)

    greet(partner, ea)
    greet(across, ea)
    for step in range(1, SHARE):
        greet(gx, base + lax.rem(place + step, SHARE))

    @pl.when(ea > 0)
    def _():
        greet(gx, ea - 1)

    @pl.when(ea < count - 1)
    def _():
        greet(gx, ea + 1)

    waits = 1 + SHARE + jnp.where(ea > 0, 1, 0) + jnp.where(ea < count - 1, 1, 0)

    row = lax.broadcasted_iota(jnp.int32, (N, N), 0)
    column = lax.broadcasted_iota(jnp.int32, (N, N), 1)
    energy = ENERGY_LOW + ENERGY_SPAN * (ea.astype(jnp.float32) + 0.5) / count
    first = jnp.where(gx == 0, 1.0, 0.0)
    final = jnp.where(gx == 3, 1.0, 0.0)
    on_diagonal = row == column
    load_diag.wait()
    load_sigma.wait()
    load_rates.wait()
    rate = BROADENING + (first * rates[0] + final * rates[1])
    own[0] = jnp.where(on_diagonal, energy, 0.0) - diag[0, 0] - sigma[0, 0, 0]
    own[1] = jnp.where(on_diagonal, rate, 0.0) - diag[1, 0] - sigma[1, 0, 0]
    work[...] = own[...]
    load_coupling.wait()
    pl.semaphore_wait(barrier, waits)
    send_piece.start()
    send_near.start()

    @pl.when(even)
    def _():
        store(step_in, adjoint((coupling[0, 0], coupling[1, 0])))
        store(step_out, (coupling[0, 0], coupling[1, 0]))

    def level(number, carry):
        def share_coupling():
            @pl.when(number == 0)
            def _():
                send_piece.wait_recv()
                for step in range(1, SHARE):
                    hand_on(step, place).start()

        invert(work, share_coupling)

        @pl.when(number == 0)
        def _():
            for step in range(1, SHARE):
                hand_on(step, lax.rem(place + SHARE - step, SHARE)).wait_recv()

            @pl.when(odd)
            def _():
                store(step_in, pair_of(link))
                store(step_out, adjoint(pair_of(link)))

            send_near.wait_send()
            g = pair_of(work)
            store(own, g)
            through = multiply(pair_of(step_in), g)
            store(reached, through)
            part = multiply(through, pair_of(step_out))
            send_near.wait_recv()
            pivot = subtract(pair_of(near), part)
            store(work, pivot)

            @pl.when(outer)
            def _():
                store(sent, pivot)
                send_mid.start()
                store(mid, pivot)

            @pl.when(gx == 0)
            def _():
                store(bridge, pair_of(link))

            @pl.when(gx == 1)
            def _():
                store(bridge, (coupling[0, 0], coupling[1, 0]))

            @pl.when(left)
            def _():
                store(bridge_h, adjoint(pair_of(bridge)))

            @pl.when(inner)
            def _():
                store(step_out, multiply(g, pair_of(step_out)))

        @pl.when(number == 1)
        def _():
            @pl.when(inner)
            def _():
                change = multiply(multiply(pair_of(step_out), pair_of(work)), pair_of(reached))
                store(work, addition(pair_of(own), change))

            @pl.when(outer)
            def _():
                send_mid.wait_send()

            @pl.when(left)
            def _():
                store(sent, multiply(pair_of(bridge_h), multiply(pair_of(work), pair_of(bridge))))

            @pl.when(right)
            def _():
                store(sent, pair_of(work))

            send_across.start()

            @pl.when(outer)
            def _():
                store(step_out, multiply(pair_of(own), pair_of(step_out)))

            @pl.when(inner)
            def _():
                send_mid.wait_recv()

            send_across.wait_recv()

        @pl.when((number == 1) & left)
        def _():
            reach = multiply(multiply(pair_of(bridge), pair_of(far)), pair_of(bridge_h))
            store(work, subtract(pair_of(mid), reach))

        @pl.when((number == 1) & right)
        def _():
            store(work, subtract(pair_of(mid), pair_of(far)))

        return carry

    lax.fori_loop(0, 3, level, 0)

    @pl.when(outer)
    def _():
        change = multiply(multiply(pair_of(step_out), pair_of(work)), pair_of(reached))
        store(last, addition(pair_of(own), change))

    @pl.when(inner)
    def _():
        store(last, pair_of(work))

    @pl.when(ea < count - 1)
    def _():
        send_up.start()

    @pl.when(ea > 0)
    def _():
        send_down.start()

    @pl.when(ea == 0)
    def _():
        before[...] = jnp.zeros_like(before)

    @pl.when(ea == count - 1)
    def _():
        after[...] = jnp.zeros_like(after)

    send_piece.wait_send()
    for step in range(1, SHARE):
        hand_on(step, place).wait_send()
    send_across.wait_send()
    load_form.wait()

    @pl.when(ea > 0)
    def _():
        send_up.wait_recv()

    @pl.when(ea < count - 1)
    def _():
        send_down.wait_recv()

    for c in range(2):
        out_ref[c, 0, 0] = form[...] * (before[c] + after[c])

    @pl.when(ea < count - 1)
    def _():
        send_up.wait_send()

    @pl.when(ea > 0)
    def _():
        send_down.wait_send()


def per_device(ham_diag, ham_coupling, sigma_prev, phonon_form, contact_rate):
    operands = (ham_diag, ham_coupling, sigma_prev, phonon_form, contact_rate)
    block = pltpu.VMEM((2, N, N), jnp.float32)
    return pl.pallas_call(
        kernel,
        out_shape=jax.ShapeDtypeStruct(sigma_prev.shape, jnp.float32),
        in_specs=[pl.BlockSpec(memory_space=pl.ANY)] * 5,
        out_specs=pl.BlockSpec(memory_space=pltpu.VMEM),
        scratch_shapes=[pltpu.VMEM(x.shape, jnp.float32) for x in operands]
        + [block] * 15
        + [pltpu.SemaphoreType.DMA((n,)) for n in (5, 6, 6, SHARE, SHARE)],
        compiler_params=pltpu.CompilerParams(
            collective_id=0, has_side_effects=True, vmem_limit_bytes=60 << 20
        ),
        name="born_update",
    )(*operands)


def solution(mesh):
    placed = (
        P(None, "gx", None, None),
        P(None, "gx", None, None),
        P(None, "gx", "ea", None, None),
        P(),
        P(None, "ea", None),
    )
    return jax.shard_map(
        per_device,
        mesh=mesh,
        in_specs=placed,
        out_specs=P(None, "gx", "ea", None, None),
        check_vma=False,
    )
```

time: 55 us -> 49 us (0.89)
  the two profiles are of different devices: /device:TPU:40 before, /device:TPU:24 now
where the time goes in v2:
time: 49 us; the launch traced here: 48.9 us
  Pallas kernels  47.3 us (97%)
  local copies, waits for them, and re-layouts  1.57 us (3%)
    pallas_call x1, Pallas kernels, per_device(): pl.pallas_call(kernel, out_shape=jax.ShapeDtypeStruct(sigma_prev.shape, j...  47.3 us
    unnamed x1, local copies, waits for them, and re-layouts  1.57 us

profile of v2, /device:TPU:24, one launch (start us, length us, event | category | flops | bytes accessed | tf_op | source)
XLA Modules:
  0.0 48.9 jit_solution(12355498492078247146)
XLA Ops:
  0.0 47.3 %born_update.1 = f32[2,1,1,128,128]{4,3,2,1,0:T(8,128)} custom-call(f32[2,1,128,128]{3,2,1,0:T(8,128)} %diag_hbm.1, f32[2,1,128,128]{3,2,1,0:T(8,128)} %coupling_hbm.1, f32[2,1,1,128,128]{4,3,2,1,0:T(8,128)} %sigma_hbm.1, f32[128,128]{1,0:T(8,128)} %form_hbm.1, f32[2,1,128]{2,1,0:T(1,128)} %rate_hbm.1), custom_call_target="tpu_custom_call" | custom-call | tf_op jit(solution)/shard_map/born_update/pallas_call | solution.py:420
  47.3 1.6 %copy.7 = f32[2,1,1,128,128]{4,3,2,1,0:T(8,128)} copy(f32[2,1,1,128,128]{4,3,2,1,0:T(8,128)} %born_update.1) | data formatting | bytes 262144

commit v3 on v2

--- a/solution.py
+++ b/solution.py
@@ -122,12 +122,12 @@
     return jnp.where(inside, 0.0, rows[0]), jnp.where(inside, 0.0, rows[1])
 
 
-def invert(ref, halfway):
+def invert(ref, between=None):
     groups = N // 8
     a = [(ref[0, 8 * g : 8 * g + 8, :], ref[1, 8 * g : 8 * g + 8, :]) for g in range(groups)]
     for s in range(groups // 2):
-        if s == 4:
-            halfway()
+        if between and s == 6:
+            between()
         g0, g1 = 2 * s, 2 * s + 1
         ahead = [] if s == groups // 2 - 1 else [g1 + 1, g1 + 2]
         old = list(a)
@@ -164,9 +164,9 @@
 
 
 def kernel(
-    diag_hbm, coupling_hbm, sigma_hbm, form_hbm, rate_hbm, out_ref,
-    diag, coupling, sigma, form, rates,
-    own, work, near, link, mid, bridge, bridge_h, step_in, step_out, reached, sent, far, last, before, after,
+    diag_hbm, coupling_hbm, sigma_hbm, rate_hbm, out_ref,
+    diag, coupling, sigma, rates,
+    own, held, work, near, link, mid, bridge, bridge_h, step_in, step_out, onward, reached, sent, far, last, before, after,
     load_sem, send_sem, recv_sem, pass_sem, piece_sem,
 ):
     gx = lax.axis_index("gx")
@@ -190,8 +190,7 @@
     load_sigma = load(1, sigma_hbm, sigma)
     load_rates = load(2, rate_hbm, rates)
     load_coupling = load(3, coupling_hbm, coupling)
-    load_form = load(4, form_hbm, form)
-    for one_load in (load_diag, load_sigma, load_rates, load_coupling, load_form):
+    for one_load in (load_diag, load_sigma, load_rates, load_coupling):
         one_load.start()
 
     def copy(src, dst, at, to_gx, to_ea):
@@ -209,10 +208,9 @@
 
     send_near = copy(own, near, 0, partner, ea)
     send_piece = copy(piece(coupling.at[:, 0], place), piece(link, place), 1, partner, ea)
-    send_mid = copy(sent, mid, 2, partner, ea)
-    send_across = copy(sent, far, 3, across, ea)
-    send_up = copy(last, before, 4, gx, lax.rem(ea + 1, count))
-    send_down = copy(last, after, 5, gx, lax.rem(ea + count - 1, count))
+    send_across = copy(sent, far, 2, across, ea)
+    send_up = copy(last, before, 3, gx, lax.rem(ea + 1, count))
+    send_down = copy(last, after, 4, gx, lax.rem(ea + count - 1, count))
 
     def hand_on(step, owner):
         return pltpu.make_async_remote_copy(
@@ -267,68 +265,61 @@
         store(step_in, adjoint((coupling[0, 0], coupling[1, 0])))
         store(step_out, (coupling[0, 0], coupling[1, 0]))
 
+    def share_coupling():
+        send_piece.wait_recv()
+        for step in range(1, SHARE):
+            hand_on(step, place).start()
+
+    invert(work, share_coupling)
+
+    for step in range(1, SHARE):
+        hand_on(step, lax.rem(place + SHARE - step, SHARE)).wait_recv()
+
+    @pl.when(odd)
+    def _():
+        store(step_in, pair_of(link))
+        store(step_out, adjoint(pair_of(link)))
+
+    @pl.when(gx == 0)
+    def _():
+        store(bridge, pair_of(link))
+
+    @pl.when(gx == 1)
+    def _():
+        store(bridge, (coupling[0, 0], coupling[1, 0]))
+
+    @pl.when(left)
+    def _():
+        store(bridge_h, adjoint(pair_of(bridge)))
+
+    g = pair_of(work)
+    through = multiply(pair_of(step_in), g)
+    store(reached, through)
+    part = multiply(through, pair_of(step_out))
+    send_near.wait_recv()
+    pivot = subtract(pair_of(near), part)
+    store(held, g)
+    store(work, pivot)
+
+    @pl.when(outer)
+    def _():
+        store(mid, pivot)
+
+    @pl.when(inner)
+    def _():
+        store(onward, multiply(pair_of(held), pair_of(step_out)))
+
     def level(number, carry):
-        def share_coupling():
-            @pl.when(number == 0)
-            def _():
-                send_piece.wait_recv()
-                for step in range(1, SHARE):
-                    hand_on(step, place).start()
-
-        invert(work, share_coupling)
-
-        @pl.when(number == 0)
-        def _():
-            for step in range(1, SHARE):
-                hand_on(step, lax.rem(place + SHARE - step, SHARE)).wait_recv()
-
-            @pl.when(odd)
-            def _():
-                store(step_in, pair_of(link))
-                store(step_out, adjoint(pair_of(link)))
-
-            send_near.wait_send()
-            g = pair_of(work)
-            store(own, g)
-            through = multiply(pair_of(step_in), g)
-            store(reached, through)
-            part = multiply(through, pair_of(step_out))
-            send_near.wait_recv()
-            pivot = subtract(pair_of(near), part)
-            store(work, pivot)
-
-            @pl.when(outer)
-            def _():
-                store(sent, pivot)
-                send_mid.start()
-                store(mid, pivot)
-
-            @pl.when(gx == 0)
-            def _():
-                store(bridge, pair_of(link))
-
-            @pl.when(gx == 1)
-            def _():
-                store(bridge, (coupling[0, 0], coupling[1, 0]))
-
-            @pl.when(left)
-            def _():
-                store(bridge_h, adjoint(pair_of(bridge)))
-
+        @pl.when(inner | (number != 2))
+        def _():
+            invert(work)
+
+        @pl.when(number == 1)
+        def _():
             @pl.when(inner)
             def _():
-                store(step_out, multiply(g, pair_of(step_out)))
-
-        @pl.when(number == 1)
-        def _():
-            @pl.when(inner)
-            def _():
-                change = multiply(multiply(pair_of(step_out), pair_of(work)), pair_of(reached))
-                store(work, addition(pair_of(own), change))
-
-            @pl.when(outer)
-            def _():
-                send_mid.wait_send()
+                change = multiply(multiply(pair_of(onward), pair_of(work)), pair_of(reached))
+                store(work, addition(pair_of(held), change))
 
             @pl.when(left)
             def _():
@@ -342,31 +333,38 @@
 
             @pl.when(outer)
             def _():
-                store(step_out, multiply(pair_of(own), pair_of(step_out)))
+                store(onward, multiply(pair_of(held), pair_of(step_out)))
 
             @pl.when(inner)
             def _():
-                send_mid.wait_recv()
-
+                store(work, pair_of(near))
+
+        @pl.when(inner & (number == 2))
+        def _():
+            part = multiply(multiply(pair_of(step_out), pair_of(work)), pair_of(step_in))
+            store(mid, subtract(pair_of(own), part))
+
+        @pl.when(number == 2)
+        def _():
             send_across.wait_recv()
 
-        @pl.when((number == 1) & left)
+        @pl.when((number == 2) & left)
         def _():
             reach = multiply(multiply(pair_of(bridge), pair_of(far)), pair_of(bridge_h))
             store(work, subtract(pair_of(mid), reach))
 
-        @pl.when((number == 1) & right)
+        @pl.when((number == 2) & right)
         def _():
             store(work, subtract(pair_of(mid), pair_of(far)))
 
         return carry
 
-    lax.fori_loop(0, 3, level, 0)
+    lax.fori_loop(1, 4, level, 0)
 
     @pl.when(outer)
     def _():
-        change = multiply(multiply(pair_of(step_out), pair_of(work)), pair_of(reached))
-        store(last, addition(pair_of(own), change))
+        change = multiply(multiply(pair_of(onward), pair_of(work)), pair_of(reached))
+        store(last, addition(pair_of(held), change))
 
     @pl.when(inner)
     def _():
@@ -388,11 +386,11 @@
     def _():
         after[...] = jnp.zeros_like(after)
 
+    send_near.wait_send()
     send_piece.wait_send()
     for step in range(1, SHARE):
         hand_on(step, place).wait_send()
     send_across.wait_send()
-    load_form.wait()
 
     @pl.when(ea > 0)
     def _():
@@ -403,7 +401,7 @@
         send_down.wait_recv()
 
     for c in range(2):
-        out_ref[c, 0, 0] = form[...] * (before[c] + after[c])
+        out_ref[c, 0, 0] = before[c] + after[c]
 
     @pl.when(ea < count - 1)
     def _():
@@ -415,21 +413,22 @@
 
 
 def per_device(ham_diag, ham_coupling, sigma_prev, phonon_form, contact_rate):
-    operands = (ham_diag, ham_coupling, sigma_prev, phonon_form, contact_rate)
+    operands = (ham_diag, ham_coupling, sigma_prev, contact_rate)
     block = pltpu.VMEM((2, N, N), jnp.float32)
-    return pl.pallas_call(
+    total = pl.pallas_call(
         kernel,
         out_shape=jax.ShapeDtypeStruct(sigma_prev.shape, jnp.float32),
-        in_specs=[pl.BlockSpec(memory_space=pl.ANY)] * 5,
+        in_specs=[pl.BlockSpec(memory_space=pl.ANY)] * 4,
         out_specs=pl.BlockSpec(memory_space=pltpu.VMEM),
         scratch_shapes=[pltpu.VMEM(x.shape, jnp.float32) for x in operands]
-        + [block] * 15
-        + [pltpu.SemaphoreType.DMA((n,)) for n in (5, 6, 6, SHARE, SHARE)],
+        + [block] * 17
+        + [pltpu.SemaphoreType.DMA((n,)) for n in (4, 5, 5, SHARE, SHARE)],
         compiler_params=pltpu.CompilerParams(
-            collective_id=0, has_side_effects=True, vmem_limit_bytes=60 << 20
+            collective_id=0, has_side_effects=True, vmem_limit_bytes=(53 << 20) + (800 << 10)
         ),
         name="born_update",
     )(*operands)
+    return phonon_form * total
 
 
 def solution(mesh):

time: 49 us -> 48.4 us (0.988)
  local copies, waits for them, and re-layouts: 1.57 us -> 0.68 us
  other arithmetic: 0 us -> 0.67 us
    unnamed x1 -> x4, local copies, waits for them, and re-layouts: 1.57 us -> 0.68 us
    mul x0 -> x1, other arithmetic: none -> 0.67 us  [per_device(): return phonon_form * total]
where the time goes in v3:
time: 48.4 us; the launch traced here: 48.2 us
  Pallas kernels  46.9 us (97%)
  local copies, waits for them, and re-layouts  0.68 us (1%)
  other arithmetic  0.67 us (1%)
    pallas_call x1, Pallas kernels, per_device(): pl.pallas_call(kernel, out_shape=jax.ShapeDtypeStruct(sigma_prev.shape, j...  46.9 us

profile of v3, /device:TPU:24, one launch (start us, length us, event | category | flops | bytes accessed | tf_op | source)
XLA Modules:
  0.0 48.2 jit_solution(13621198266939895424)
XLA Ops:
  0.0 0.0 copy-start
  0.0 0.7 %copy-done = f32[2,1,128]{2,1,0:T(1,128)S(1)} copy-done((f32[2,1,128]{2,1,0:T(1,128)S(1)}, f32[2,1,128]{2,1,0:T(1,128)}, u32[]{:S(2)}) %copy-start) | copy-done | bytes 1048
  0.7 0.0 copy-start.1
  0.7 46.9 %born_update.1 = f32[2,1,1,128,128]{4,3,2,1,0:T(8,128)S(1)} custom-call(f32[2,1,128,128]{3,2,1,0:T(8,128)} %diag_hbm.1, f32[2,1,128,128]{3,2,1,0:T(8,128)} %coupling_hbm.1, f32[2,1,1,128,128]{4,3,2,1,0:T(8,128)} %sigma_hbm.1, f32[2,1,128]{2,1,0:T(1,128)S(1)} %copy-done), custom_call_target="tpu_custom_call" | custom-call | tf_op jit(solution)/shard_map/born_update/pallas_call | solution.py:418
  47.5 0.0 copy-done.1
  47.6 0.7 %broadcast_multiply_fusion = f32[2,1,1,128,128]{4,3,2,1,0:T(8,128)} fusion(f32[2,1,1,128,128]{4,3,2,1,0:T(8,128)S(1)} %born_update.1, f32[128,128]{1,0:T(8,128)S(1)} %copy-done.1), kind=kLoop, calls=%fused_computation | loop fusion | flops 32768 | bytes 327680 | tf_op jit(solution)/shard_map/mul | solution.py:431
Async XLA Ops:
  0.0 0.7 %copy-start = (f32[2,1,128]{2,1,0:T(1,128)S(1)}, f32[2,1,128]{2,1,0:T(1,128)}, u32[]{:S(2)}) copy-start(f32[2,1,128]{2,1,0:T(1,128)} %rate_hbm.1) | copy-start | bytes 3076
  0.7 46.9 %copy-start.1 = (f32[128,128]{1,0:T(8,128)S(1)}, f32[128,128]{1,0:T(8,128)}, u32[]{:S(2)}) copy-start(f32[128,128]{1,0:T(8,128)} %param.8) | copy-start | bytes 196612

commit v4 on v3

--- a/solution.py
+++ b/solution.py
@@ -10,7 +10,7 @@
 ENERGY_SPAN = 4.0
 N = 128
 TILE = (8, 128)
-SHARE = 8
+SHARE = 2
 ROWS = N // SHARE
 MESH = pl.DeviceIdType.MESH
 
@@ -122,12 +122,10 @@
     return jnp.where(inside, 0.0, rows[0]), jnp.where(inside, 0.0, rows[1])
 
 
-def invert(ref, between=None):
+def invert(ref):
     groups = N // 8
     a = [(ref[0, 8 * g : 8 * g + 8, :], ref[1, 8 * g : 8 * g + 8, :]) for g in range(groups)]
     for s in range(groups // 2):
-        if between and s == 6:
-            between()
         g0, g1 = 2 * s, 2 * s + 1
         ahead = [] if s == groups // 2 - 1 else [g1 + 1, g1 + 2]
         old = list(a)
@@ -265,12 +263,10 @@
         store(step_in, adjoint((coupling[0, 0], coupling[1, 0])))
         store(step_out, (coupling[0, 0], coupling[1, 0]))
 
-    def share_coupling():
-        send_piece.wait_recv()
-        for step in range(1, SHARE):
-            hand_on(step, place).start()
-
-    invert(work, share_coupling)
+    invert(work)
+    send_piece.wait_recv()
+    for step in range(1, SHARE):
+        hand_on(step, place).start()
 
     for step in range(1, SHARE):
         hand_on(step, lax.rem(place + SHARE - step, SHARE)).wait_recv()

time: 48.4 us -> 45.2 us (0.934)
  the two profiles are of different devices: /device:TPU:24 before, /device:TPU:56 now
where the time goes in v4:
time: 45.2 us; the launch traced here: 45.1 us
  Pallas kernels  43.7 us (97%)
  local copies, waits for them, and re-layouts  0.68 us (2%)
  other arithmetic  0.67 us (1%)
    pallas_call x1, Pallas kernels, per_device(): pl.pallas_call(kernel, out_shape=jax.ShapeDtypeStruct(sigma_prev.shape, j...  43.7 us

profile of v4, /device:TPU:56, one launch (start us, length us, event | category | flops | bytes accessed | tf_op | source)
XLA Modules:
  0.0 45.1 jit_solution(12942159750506086638)
XLA Ops:
  0.0 0.0 copy-start
  0.0 0.7 %copy-done = f32[2,1,128]{2,1,0:T(1,128)S(1)} copy-done((f32[2,1,128]{2,1,0:T(1,128)S(1)}, f32[2,1,128]{2,1,0:T(1,128)}, u32[]{:S(2)}) %copy-start) | copy-done | bytes 1048
  0.7 0.0 copy-start.1
  0.7 43.7 %born_update.1 = f32[2,1,1,128,128]{4,3,2,1,0:T(8,128)S(1)} custom-call(f32[2,1,128,128]{3,2,1,0:T(8,128)} %diag_hbm.1, f32[2,1,128,128]{3,2,1,0:T(8,128)} %coupling_hbm.1, f32[2,1,1,128,128]{4,3,2,1,0:T(8,128)} %sigma_hbm.1, f32[2,1,128]{2,1,0:T(1,128)S(1)} %copy-done), custom_call_target="tpu_custom_call" | custom-call | tf_op jit(solution)/shard_map/born_update/pallas_call | solution.py:414
  44.4 0.0 copy-done.1
  44.4 0.7 %broadcast_multiply_fusion = f32[2,1,1,128,128]{4,3,2,1,0:T(8,128)} fusion(f32[2,1,1,128,128]{4,3,2,1,0:T(8,128)S(1)} %born_update.1, f32[128,128]{1,0:T(8,128)S(1)} %copy-done.1), kind=kLoop, calls=%fused_computation | loop fusion | flops 32768 | bytes 327680 | tf_op jit(solution)/shard_map/mul | solution.py:427
Async XLA Ops:
  0.0 0.7 %copy-start = (f32[2,1,128]{2,1,0:T(1,128)S(1)}, f32[2,1,128]{2,1,0:T(1,128)}, u32[]{:S(2)}) copy-start(f32[2,1,128]{2,1,0:T(1,128)} %rate_hbm.1) | copy-start | bytes 3076
  0.7 43.7 %copy-start.1 = (f32[128,128]{1,0:T(8,128)S(1)}, f32[128,128]{1,0:T(8,128)}, u32[]{:S(2)}) copy-start(f32[128,128]{1,0:T(8,128)} %param.8) | copy-start | bytes 196612
